TPU v7x, 32 devices: a whole 2x2x4 slice. The times are simulated.
32 devices in a mesh: dp: 4 (over z), expert: 4 (over y, x), tensor: 2 (over core).
Axes of the slice: x: 2, y: 2, z: 4, core: 2. Of those that a mesh axis runs over, the one named last changes fastest.
Arguments:
- hidden_in: bfloat16 [4096, 2048], P(('dp', 'expert')), may hold values from -6 to 6
- query: bfloat16 [4096, 2048], P(('dp', 'expert'), 'tensor'), may hold values from -26 to 26
- keys: bfloat16 [4096, 2048], P(('dp', 'expert'), 'tensor'), may hold values from -26 to 26
- values: bfloat16 [4096, 2048], P(('dp', 'expert'), 'tensor'), may hold values from -6 to 6
- out_proj: bfloat16 [2048, 2048], P('tensor'), may hold values from -0.125 to 0.125
- norm_gain: bfloat16 [2048], replicated, may hold values from 0.25 to 1.75
- routes: int32 [4096, 2], P(('dp', 'expert')), may hold values from 0 to 3, all different within a row; in each aligned block of 256 rows (0 to 255, 256 to 511, ...) at most 144 rows name the same one
- gates: float32 [4096, 2], P(('dp', 'expert')), may hold values from 0.2 to 1
- w_gate: bfloat16 [4, 2048, 5504], P('expert', 'dp', 'tensor'), may hold values from -0.125 to 0.125
- w_up: bfloat16 [4, 2048, 5504], P('expert', 'dp', 'tensor'), may hold values from -0.125 to 0.125
- w_down_t: bfloat16 [4, 2048, 5504], P('expert', 'dp', 'tensor'), may hold values from -0.078125 to 0.078125
Outputs:
- layer_out: bfloat16 [4096, 2048], P(('dp', 'expert'), 'tensor')
Inputs may be any that keep to these rules, and one draw needn't show every extreme that they name: `routes`: each row names 2 different experts; in the 256 rows of one block of consecutive tokens no expert is named more than 144 times, a bound that some block reaches.
All inputs are finite; a program needn't handle non-finite values.
Results may differ from a plain program's by a relative error of at most 0.0095.
Values may be sent and summed in bfloat16 or wider, within the bound.
A program may use at most 128 MiB of HBM per device.

v0:
```python
import jax
import jax.numpy as jnp
from jax import lax
from jax.sharding import PartitionSpec as P

HDIM = 128
EPSILON = 1e-05
NEGATIVE = -1e30


def slot_table(block_routes, experts, capacity):
    flat_routes = block_routes.reshape(-1)
    onehot = (flat_routes[:, None] == jnp.arange(experts, dtype=jnp.int32)[None, :]).astype(
        jnp.int32
    )
    rank_table = jnp.cumsum(onehot, axis=0) - 1
    slot_index = jnp.sum(rank_table * onehot, axis=1)
    return flat_routes * capacity + slot_index


def local(
    hidden_in, query, keys, values, out_proj, norm_gain, routes, gates, w_gate, w_up, w_down_t
):
    tok_rows, feature_width = hidden_in.shape
    head_cols = query.shape[1]
    head_count = head_cols // HDIM
    experts = lax.axis_size("expert")
    capacity = 9 * tok_rows // (4 * experts)
    tensor_count = lax.axis_size("tensor")
    slice_width = feature_width // tensor_count
    tensor_index = lax.axis_index("tensor")
    query_pos = lax.axis_index("expert") * tok_rows + jnp.arange(tok_rows, dtype=jnp.int32)
    score_scale = 1.0 / HDIM**0.5
    queries = query.astype(jnp.float32).reshape(tok_rows, head_count, HDIM)
    maxima = jnp.full((head_count, tok_rows), NEGATIVE, jnp.float32)
    key_rows = lax.all_gather(keys, "expert", axis=0, tiled=True)
    value_rows = lax.all_gather(values, "expert", axis=0, tiled=True)
    count_rows = key_rows.shape[0]
    key_pos = jnp.arange(count_rows, dtype=jnp.int32)
    key_part = key_rows.astype(jnp.float32).reshape(count_rows, head_count, HDIM)
    value_part = value_rows.astype(jnp.float32).reshape(count_rows, head_count, HDIM)
    scores = jnp.einsum("qhd,khd->hqk", queries, key_part) * score_scale
    causal = (query_pos[:, None] >= key_pos[None, :])[None]
    scores = jnp.where(causal, scores, NEGATIVE)
    new_max = jnp.maximum(maxima, jnp.max(scores, axis=-1))
    weights_now = jnp.where(causal, jnp.exp(scores - new_max[..., None]), 0.0)
    totals = jnp.sum(weights_now, axis=-1)
    weighted = jnp.einsum("hqk,khd->hqd", weights_now, value_part)
    maxima, totals, weighted = (new_max, totals, weighted)
    context = weighted / totals[..., None]
    context = jnp.transpose(context, (1, 0, 2)).reshape(tok_rows, head_cols).astype(jnp.bfloat16)
    attended = lax.psum(
        jnp.dot(context, out_proj, preferred_element_type=jnp.float32).astype(jnp.bfloat16),
        "tensor",
    ).astype(jnp.float32)
    residual = hidden_in.astype(jnp.float32) + attended
    mean_square = jnp.mean(residual * residual, axis=-1, keepdims=True)
    normed = (residual * lax.rsqrt(mean_square + EPSILON) * norm_gain.astype(jnp.float32)).astype(
        jnp.bfloat16
    )
    targets = slot_table(routes, experts, capacity)
    doubled = jnp.repeat(normed, routes.shape[1], axis=0)
    send_rows = (
        jnp.zeros((experts * capacity, feature_width), jnp.bfloat16).at[targets].set(doubled)
    )
    send_rows = send_rows.reshape(experts, capacity, feature_width)
    arrived = lax.all_to_all(send_rows, "expert", split_axis=0, concat_axis=0, tiled=True)
    slot_rows = arrived.reshape(experts * capacity, feature_width)
    gate_full, up_full, down_full = (
        lax.all_gather(w_gate, "dp", axis=1, tiled=True),
        lax.all_gather(w_up, "dp", axis=1, tiled=True),
        lax.all_gather(w_down_t, "dp", axis=1, tiled=True),
    )
    gate_out = jnp.dot(slot_rows, gate_full[0], preferred_element_type=jnp.float32)
    up_out = jnp.dot(slot_rows, up_full[0], preferred_element_type=jnp.float32)
    hidden = (jax.nn.silu(gate_out) * up_out).astype(jnp.bfloat16)
    partial_value = lax.dot_general(
        hidden, down_full[0], (((1,), (1,)), ((), ())), preferred_element_type=jnp.float32
    )
    rounded = partial_value.astype(jnp.bfloat16)
    own_slice = lax.dynamic_slice_in_dim(residual, tensor_index * slice_width, slice_width, 1)
    summed = lax.psum_scatter(
        lax.optimization_barrier(rounded).astype(jnp.float32).astype(jnp.bfloat16),
        "tensor",
        scatter_dimension=1,
        tiled=True,
    ).astype(jnp.float32)
    returned = lax.all_to_all(
        summed.reshape(experts, capacity, slice_width).astype(jnp.bfloat16),
        "expert",
        split_axis=0,
        concat_axis=0,
        tiled=True,
    ).astype(jnp.float32)
    fetched = returned.reshape(experts * capacity, slice_width)[targets].reshape(
        tok_rows, routes.shape[1], slice_width
    )
    mixture = jnp.sum(gates[:, :, None] * fetched, axis=1)
    return (own_slice + mixture).astype(jnp.bfloat16)


def solution(mesh):
    in_specs = (
        P(("dp", "expert"), None),
        P(("dp", "expert"), "tensor"),
        P(("dp", "expert"), "tensor"),
        P(("dp", "expert"), "tensor"),
        P("tensor", None),
        P(),
        P(("dp", "expert"), None),
        P(("dp", "expert"), None),
        P("expert", "dp", "tensor"),
        P("expert", "dp", "tensor"),
        P("expert", "dp", "tensor"),
    )
    out_specs = P(("dp", "expert"), "tensor")
    return jax.shard_map(local, mesh=mesh, in_specs=in_specs, out_specs=out_specs, check_vma=False)
```

profile of v0, /device:TPU:0, one launch (start us, length us, event | category | flops | bytes accessed | tf_op | source)
XLA Modules:
  0.0 761.1 jit_solution(10035004202063859870)
XLA Ops:
  7.4 0.0 copy-start
  7.4 0.0 all-gather.6.cloned.1.call-start
  7.4 2.1 copy.15
  9.5 0.0 all-gather.6.cloned.1.call-update
  9.5 0.0 all-gather.8.cloned.1.call-start
  9.5 0.7 all-gather.8.cloned.1.call-update
  10.2 0.0 all-reduce.2.cloned.1.call-start
  10.3 0.2 iota_compare_fusion
  10.5 37.4 %all-gather.6.cloned.1.call-done = bf16[1024,1024]{0,1:T(8,128)(2,1)} async-done(((bf16[256,1024]{0,1:T(8,128)(2,1)}), bf16[1024,1024]{0,1:T(8,128)(2,1)}) %all-gather.6.cloned.1.call-update) | async-done | bytes 2097168 | tf_op jit(solution)/shard_map/all_gather | solution.py:36
  47.9 0.0 copy-done
  47.9 3.4 fusion.6
  51.4 3.2 copy-done.2
  54.6 2.6 fusion.7
  57.2 27.9 %all-gather.8.cloned.1.call-done = bf16[1024,1024]{1,0:T(8,128)(2,1)} async-done(((bf16[256,1024]{1,0:T(8,128)(2,1)}), bf16[1024,1024]{1,0:T(8,128)(2,1)}) %all-gather.8.cloned.1.call-update) | async-done | bytes 2097168 | tf_op jit(solution)/shard_map/all_gather | solution.py:37
  85.1 2.9 copy.18
  88.0 0.0 copy-start.10
  88.0 5.9 divide_convert_fusion
  93.9 0.0 copy-done.10
  93.9 2.3 convolution_convert_fusion
  96.1 0.0 all-reduce.2.cloned.1.call-update
  96.1 0.0 all-gather.10.cloned.1.call-start
  96.2 0.5 all-gather.10.cloned.1.call-update
  96.7 0.0 copy-start.7
  96.7 0.0 copy-start.8
  96.7 0.0 copy-start.4
  96.8 0.0 all-gather.12.cloned.1.call-start
  96.8 0.5 all-gather.12.cloned.1.call-update
  97.3 0.0 all-gather.14.cloned.1.call-start
  97.4 0.5 all-gather.14.cloned.1.call-update
  97.9 0.2 reduce-scatter.2.cloned.1.call-start
  98.2 0.1 copy.21
  98.3 0.1 eq.29
  98.5 0.1 eq.25
  98.6 1.2 reduce-window.6
  99.9 0.2 slice_reduce_fusion
  100.1 0.2 reduce-window.9
  100.3 0.1 copy.20
  100.4 0.1 mul.72
  100.6 0.1 add_bitcast_fusion
  100.7 15.2 %all-reduce.2.cloned.1.call-done = bf16[256,2048]{1,0:T(8,128)(2,1)} async-done(((bf16[256,2048]{1,0:T(8,128)(2,1)}), bf16[256,2048]{1,0:T(8,128)(2,1)}) %all-reduce.2.cloned.1.call-update) | async-done | bytes 1048592 | tf_op jit(solution)/shard_map/psum | solution.py:52
  115.9 0.0 copy-done.4
  115.9 3.0 convert_add_fusion
  118.9 0.5 multiply_convert_fusion.1
  119.4 1.3 broadcast_in_dim.43
  120.7 2.2 reshape.140
  122.9 5.3 scatter_custom_fusion
  128.3 32.5 %all_to_all.10 = bf16[4,144,2048]{2,1,0:T(8,128)(2,1)} all-to-all(bf16[4,144,2048]{2,1,0:T(8,128)(2,1)S(1)} %bitcast.63), channel_id=1, replica_groups=mesh['dp'=4,'expert'=4,'tensor'=2] {'expert'}, dimensions={0} | all-to-all | bytes 4718592 | tf_op jit(solution)/shard_map/all_to_all | solution.py:67
  160.7 134.2 %all-gather.10.cloned.1.call-done = bf16[1,2048,2752]{1,2,0:T(8,128)(2,1)} async-done(((bf16[1,512,2752]{1,2,0:T(8,128)(2,1)}), bf16[1,2048,2752]{1,2,0:T(8,128)(2,1)}) %all-gather.10.cloned.1.call-update) | async-done | bytes 11272208 | tf_op jit(solution)/shard_map/all_gather | solution.py:70
  294.9 13.5 %fusion.4 = f32[576,2752]{1,0:T(8,128)} fusion(bf16[576,2048]{1,0:T(8,128)(2,1)} %bitcast.64, bf16[1,2048,2752]{1,2,0:T(8,128)(2,1)} %all-gather.10.cloned.1.call-done), kind=kOutput, calls=%fused_computation.6 | convolution fusion | flops 6492782592 | bytes 19972096 | tf_op jit(solution)/shard_map/dot_general | solution.py:74
  308.4 182.9 %all-gather.12.cloned.1.call-done = bf16[1,2048,2752]{1,2,0:T(8,128)(2,1)} async-done(((bf16[1,512,2752]{1,2,0:T(8,128)(2,1)}), bf16[1,2048,2752]{1,2,0:T(8,128)(2,1)}) %all-gather.12.cloned.1.call-update) | async-done | bytes 11272208 | tf_op jit(solution)/shard_map/all_gather | solution.py:71
  491.3 196.4 %all-gather.14.cloned.1.call-done = bf16[1,2048,2752]{1,2,0:T(8,128)(2,1)} async-done(((bf16[1,512,2752]{1,2,0:T(8,128)(2,1)}), bf16[1,2048,2752]{1,2,0:T(8,128)(2,1)}) %all-gather.14.cloned.1.call-update) | async-done | bytes 11272208 | tf_op jit(solution)/shard_map/all_gather | solution.py:72
  687.6 27.1 %fusion.18 = bf16[576,2048]{1,0:T(8,128)(2,1)} fusion(bf16[1,2048,2752]{1,2,0:T(8,128)(2,1)} %all-gather.14.cloned.1.call-done, f32[576,2752]{1,0:T(8,128)} %fusion.4, bf16[576,2048]{1,0:T(8,128)(2,1)S(1)} %bitcast.65, bf16[1,2048,2752]{1,2,0:T(8,128)(2,1)} %all-gather.12.cloned.1.call-done), kind=kOutput, calls=%fused_computation.19 | convolution fusion | flops 12996255744 | bytes 33603584 | tf_op jit(solution)/shard_map/dot_general | solution.py:77
  714.7 0.0 reduce-scatter.2.cloned.1.call-update
  714.7 8.2 %reduce-scatter.2.cloned.1.call-done = bf16[576,1024]{1,0:T(8,128)(2,1)} async-done(((bf16[576,2048]{1,0:T(8,128)(2,1)}), bf16[576,1024]{1,0:T(8,128)(2,1)}) %reduce-scatter.2.cloned.1.call-update) | async-done | bytes 1179664 | tf_op jit(solution)/shard_map/reduce_scatter | solution.py:82
  723.0 4.5 all-to-all-start.1
  727.5 0.1 copy.19
  727.7 15.7 %all-to-all-done.1 = bf16[4,144,1024]{2,1,0:T(8,128)(2,1)} async-done(((bf16[4,144,1024]{2,1,0:T(8,128)(2,1)}), bf16[4,144,1024]{2,1,0:T(8,128)(2,1)}, u32[]{:S(2)}, u32[]{:S(2)}) %all-to-all-start.1) | async-done | bytes 1179680 | tf_op jit(solution)/shard_map/all_to_all | solution.py:88
  743.3 1.5 bitcast_convert_fusion
  744.9 2.7 gather_fusion
  747.6 2.5 reshape.125
  750.1 2.6 multiply_reduce_fusion
  752.8 0.0 copy-done.3
  752.8 0.9 add_convert_fusion
  753.7 0.0 copy-done.1
  (20 shorter events, 0.1 us)
Async XLA Ops:
  7.4 40.6 %copy-start = (bf16[256,1024]{1,0:T(8,128)(2,1)S(1)}, bf16[256,1024]{1,0:T(8,128)(2,1)}, u32[]{:S(2)}) copy-start(bf16[256,1024]{1,0:T(8,128)(2,1)} %param.12) | copy-start | bytes 1572868
  7.4 40.5 %all-gather.6.cloned.1.call-start = ((), (), s32[]{:S(2)}) async-start(), calls=%async_computation.3 | async-start | bytes 2621440 | tf_op jit(solution)/shard_map/all_gather | solution.py:36
  9.5 75.6 %all-gather.8.cloned.1.call-start = ((), (), s32[]{:S(2)}) async-start(), calls=%async_computation.4 | async-start | bytes 2621440 | tf_op jit(solution)/shard_map/all_gather | solution.py:37
  10.2 105.6 %all-reduce.2.cloned.1.call-start = ((), (), s32[]{:S(2)}) async-start(), calls=%async_computation.5 | async-start | bytes 2097152 | tf_op jit(solution)/shard_map/psum | solution.py:52
  51.3 3.2 copy-start.2
  88.0 5.9 copy-start.10
  96.1 198.8 %all-gather.10.cloned.1.call-start = ((), (), s32[]{:S(2)}) async-start(), calls=%async_computation.6 | async-start | bytes 14090240 | tf_op jit(solution)/shard_map/all_gather | solution.py:70
  96.7 1.4 copy-start.7
  96.7 1.9 copy-start.8
  96.7 19.1 %copy-start.4 = (bf16[256,2048]{1,0:T(8,128)(2,1)S(1)}, bf16[256,2048]{1,0:T(8,128)(2,1)}, u32[]{:S(2)}) copy-start(bf16[256,2048]{1,0:T(8,128)(2,1)} %param.11) | copy-start | bytes 3145732
  96.8 394.5 %all-gather.12.cloned.1.call-start = ((), (), s32[]{:S(2)}) async-start(), calls=%async_computation.7 | async-start | bytes 14090240 | tf_op jit(solution)/shard_map/all_gather | solution.py:71
  97.3 590.3 %all-gather.14.cloned.1.call-start = ((), (), s32[]{:S(2)}) async-start(), calls=%async_computation.8 | async-start | bytes 14090240 | tf_op jit(solution)/shard_map/all_gather | solution.py:72
  97.9 625.0 %reduce-scatter.2.cloned.1.call-start = ((), (), s32[]{:S(2)}) async-start(), calls=%async_computation.9 | async-start | bytes 3538944 | tf_op jit(solution)/shard_map/reduce_scatter | solution.py:82
  115.9 3.0 copy-start.5
  294.9 392.7 %copy-start.6 = (bf16[4,144,2048]{2,1,0:T(8,128)(2,1)S(1)}, bf16[4,144,2048]{2,1,0:T(8,128)(2,1)}, u32[]{:S(2)}) copy-start(bf16[4,144,2048]{2,1,0:T(8,128)(2,1)} %all_to_all.10) | copy-start | bytes 7077892
  714.7 12.8 %copy-start.9 = (f32[256,2]{0,1:T(2,128)S(1)}, f32[256,2]{0,1:T(2,128)}, u32[]{:S(2)}) copy-start(f32[256,2]{0,1:T(2,128)} %param.18) | copy-start | bytes 6148
  723.0 20.4 %all-to-all-start.1 = ((bf16[4,144,1024]{2,1,0:T(8,128)(2,1)}), bf16[4,144,1024]{2,1,0:T(8,128)(2,1)}, u32[]{:S(2)}, u32[]{:S(2)}) async-start(bf16[4,144,1024]{2,1,0:T(8,128)(2,1)} %bitcast.68), calls=%async_computation.2 | async-start | bytes 2359296 | tf_op jit(solution)/shard_map/all_to_all | solution.py:88
  747.6 6.2 copy-start.1
  750.1 2.7 copy-start.3
Sparse Core Ops, SparseCore 0:
  10.0 37.8 all-gather.5
  49.8 35.3 all-gather.7
  96.3 19.5 all-reduce.1
  714.8 8.0 reduce-scatter.1
Sparse Core Ops, SparseCore 1:
  98.3 196.6 all-gather.9
  296.4 194.8 all-gather.11
  492.8 194.8 all-gather.13
where the time goes:
time: 762 us; the launch traced here: 761 us
  waiting for transfers between devices  620 us (81%)
  matrix products  52.1 us (7%)
  blocking collectives  32.5 us (4%)
  local copies, waits for them, and re-layouts  23.4 us (3%)
  between operations  15.1 us (2%)
  other arithmetic  13 us (2%)
    all_gather x1, waiting for transfers between devices, local(): lax.all_gather(w_down_t, 'dp', axis=1, tiled=True)  196 us
    all_gather x1, waiting for transfers between devices, local(): lax.all_gather(w_up, 'dp', axis=1, tiled=True)  183 us
    all_gather x1, waiting for transfers between devices, local(): lax.all_gather(w_gate, 'dp', axis=1, tiled=True)  134 us
    all_gather x1, waiting for transfers between devices, local(): key_rows = lax.all_gather(keys, 'expert', axis=0, tiled=True)  37.4 us
    all_to_all x1, blocking collectives, local(): lax.all_to_all(send_rows, 'expert', split_axis=0, concat_axis=0, tiled=True)  32.5 us
    all_gather x1, waiting for transfers between devices, local(): value_rows = lax.all_gather(values, 'expert', axis=0, tiled=True)  27.9 us
    dot_general x1, matrix products, local(): lax.dot_general(hidden, down_full[0], (((1,), (1,)), ((), ())), preferred...  27.1 us
    all_to_all x1, waiting for transfers between devices, local(): lax.all_to_all(summed.reshape(experts, capacity, slice_width).astype(jnp....  15.7 us
  transfers between devices with their start and end apart: 8, of which 8 were waited for; matrix products, arithmetic and copies ran while one was open for 5% of the time, Pallas kernels for 0%

commit v1 on v0

--- a/solution.py
+++ b/solution.py
@@ -6,6 +6,27 @@
 HDIM = 128
 EPSILON = 1e-05
 NEGATIVE = -1e30
+
+
+def ring_gather(array, axis, dim):
+    size, place, span = (lax.axis_size(axis), lax.axis_index(axis), array.shape[dim])
+    right = [(i, (i + 1) % size) for i in range(size)]
+    left = [(i, (i - 1) % size) for i in range(size)]
+    filled = jnp.zeros((*array.shape[:dim], size * span, *array.shape[dim + 1 :]), array.dtype)
+    filled = lax.dynamic_update_slice_in_dim(filled, array, place * span, axis=dim)
+    from_left = from_right = array
+    halfway = size // 2
+    for step in range(1, halfway + 1):
+        from_left = lax.ppermute(from_left, axis, right)
+        filled = lax.dynamic_update_slice_in_dim(
+            filled, from_left, (place - step) % size * span, axis=dim
+        )
+        if step < size - halfway:
+            from_right = lax.ppermute(from_right, axis, left)
+            filled = lax.dynamic_update_slice_in_dim(
+                filled, from_right, (place + step) % size * span, axis=dim
+            )
+    return filled
 
 
 def slot_table(block_routes, experts, capacity):
@@ -67,7 +88,7 @@
     arrived = lax.all_to_all(send_rows, "expert", split_axis=0, concat_axis=0, tiled=True)
     slot_rows = arrived.reshape(experts * capacity, feature_width)
     gate_full, up_full, down_full = (
-        lax.all_gather(w_gate, "dp", axis=1, tiled=True),
+        ring_gather(w_gate, "dp", 1),
         lax.all_gather(w_up, "dp", axis=1, tiled=True),
         lax.all_gather(w_down_t, "dp", axis=1, tiled=True),
     )

time: 762 us -> 734 us (0.963)
  waiting for transfers between devices: 620 us -> 492 us
  starting transfers between devices: 4.97 us -> 116 us
  blocking collectives: 32.5 us -> 0 us
  local copies, waits for them, and re-layouts: 23.4 us -> 46.1 us
    ppermute x0 -> x3, waiting for transfers between devices: none -> 211 us  [the longest x2 198 us: ring_gather(): from_left = lax.ppermute(from_left, axis, right)]
    all_gather x1, waiting for transfers between devices: 196 us -> 0.01 us  [local(): lax.all_gather(w_down_t, 'dp', axis=1, tiled=True)]
    all_gather x1 -> x0, waiting for transfers between devices: 134 us -> none  [local(): lax.all_gather(w_gate, 'dp', axis=1, tiled=True)]
    ppermute x0 -> x3, starting transfers between devices: none -> 107 us  [the longest x2 105 us: ring_gather(): from_left = lax.ppermute(from_left, axis, right)]
    all_to_all x1 -> x0, blocking collectives: 32.5 us -> none  [local(): lax.all_to_all(send_rows, 'expert', split_axis=0, concat_axis=0, tiled=True)]
    psum x1, waiting for transfers between devices: 15.2 us -> 0.02 us  [local(): lax.psum(jnp.dot(context, out_proj, preferred_element_type=jnp.float32).a...]
    dynamic_update_slice x0 -> x4, local copies, waits for them, and re-layouts: none -> 15 us  [the longest x2 7.22 us: ring_gather(): lax.dynamic_update_slice_in_dim(filled, from_left, (place - step) % size...]
  transfers between devices with their start and end apart: 8 -> 11, of which waited for: 8 -> 8; matrix products, arithmetic and copies ran while one was open for 5% -> 8% of each run, Pallas kernels for 0% -> 0%
where the time goes in v1:
time: 734 us; the launch traced here: 733 us
  waiting for transfers between devices  492 us (67%)
  starting transfers between devices  116 us (16%)
  matrix products  50.8 us (7%)
  local copies, waits for them, and re-layouts  46.1 us (6%)
  between operations  14.9 us (2%)
  other arithmetic  13 us (2%)
    ppermute x2, waiting for transfers between devices, ring_gather(): from_left = lax.ppermute(from_left, axis, right)  198 us
    all_gather x1, waiting for transfers between devices, local(): lax.all_gather(w_up, 'dp', axis=1, tiled=True)  190 us
    ppermute x2, starting transfers between devices, ring_gather(): from_left = lax.ppermute(from_left, axis, right)  105 us
    all_gather x1, waiting for transfers between devices, local(): key_rows = lax.all_gather(keys, 'expert', axis=0, tiled=True)  37.4 us
    all_gather x1, waiting for transfers between devices, local(): value_rows = lax.all_gather(values, 'expert', axis=0, tiled=True)  27.9 us
    dot_general x1, matrix products, local(): lax.dot_general(hidden, down_full[0], (((1,), (1,)), ((), ())), preferred...  27.1 us
    all_to_all x1, waiting for transfers between devices, local(): lax.all_to_all(summed.reshape(experts, capacity, slice_width).astype(jnp....  15.7 us
  transfers between devices with their start and end apart: 11, of which 8 were waited for; matrix products, arithmetic and copies ran while one was open for 8% of the time, Pallas kernels for 0%

profile of v1, /device:TPU:0, one launch (start us, length us, event | category | flops | bytes accessed | tf_op | source)
XLA Modules:
  0.0 733.2 jit_solution(16798830040605215878)
XLA Ops:
  7.4 0.0 copy-start
  7.4 2.1 copy.15
  9.5 0.0 all-gather.5.cloned.1.call-update
  9.5 0.0 all-gather.7.cloned.1.call-start
  9.5 0.7 all-gather.7.cloned.1.call-update
  10.2 0.0 all-reduce.2.cloned.1.call-start
  10.3 0.2 iota_compare_fusion
  10.5 37.4 %all-gather.5.cloned.1.call-done = bf16[1024,1024]{0,1:T(8,128)(2,1)} async-done(((bf16[256,1024]{0,1:T(8,128)(2,1)}), bf16[1024,1024]{0,1:T(8,128)(2,1)}) %all-gather.5.cloned.1.call-update) | async-done | bytes 2097168 | tf_op jit(solution)/shard_map/all_gather | solution.py:57
  47.9 3.4 fusion.4
  51.4 3.2 copy-done.2
  54.6 2.6 fusion.5
  57.2 27.9 %all-gather.7.cloned.1.call-done = bf16[1024,1024]{1,0:T(8,128)(2,1)} async-done(((bf16[256,1024]{1,0:T(8,128)(2,1)}), bf16[1024,1024]{1,0:T(8,128)(2,1)}) %all-gather.7.cloned.1.call-update) | async-done | bytes 2097168 | tf_op jit(solution)/shard_map/all_gather | solution.py:58
  85.1 2.9 copy.18
  88.0 0.0 copy-start.9
  88.0 5.9 divide_convert_fusion
  93.9 2.3 convolution_convert_fusion
  96.2 0.0 all-reduce.2.cloned.1.call-update
  96.2 0.0 all-gather.11.cloned.1.call-start
  96.2 0.5 all-gather.11.cloned.1.call-update
  96.8 0.0 all-gather.9.cloned.1.call-start
  96.8 0.5 all-gather.9.cloned.1.call-update
  97.3 1.5 collective-permute-start
  98.9 2.3 collective-permute-start.1
  101.2 0.0 copy-done.6
  101.2 0.1 copy.21
  101.4 0.1 eq.33
  101.5 0.1 eq.29
  101.7 1.2 reduce-window.6
  102.9 0.2 slice_reduce_fusion
  103.1 0.2 reduce-window.9
  103.3 0.1 copy.20
  103.4 0.1 mul.84
  103.6 0.1 add_bitcast_fusion
  103.7 6.8 squeeze.17
  110.5 4.1 bitcast_dynamic-update-slice_fusion.3
  114.6 99.2 %collective-permute-done = bf16[1,512,2752]{1,2,0:T(8,128)(2,1)} collective-permute-done((bf16[1,512,2752]{1,2,0:T(8,128)(2,1)}, bf16[1,512,2752]{1,2,0:T(8,128)(2,1)}, u32[]{:S(2)}, u32[]{:S(2)}) %collective-permute-start) | collective-permute-done | bytes 2818080 | tf_op jit(solution)/shard_map/ppermute | solution.py:20
  213.8 103.6 %collective-permute-start.2 = (bf16[1,512,2752]{1,2,0:T(8,128)(2,1)}, bf16[1,512,2752]{1,2,0:T(8,128)(2,1)}, u32[]{:S(2)}, u32[]{:S(2)}) collective-permute-start(bf16[1,512,2752]{1,2,0:T(8,128)(2,1)} %collective-permute-done), channel_id=1, source_target_pairs={{0,8},{8,16},{16,24},{24,0},{1,9},{9,17},{17,25},{25,1},{2,10},{10... | collective-permute-start | bytes 8454152 | tf_op jit(solution)/shard_map/ppermute | solution.py:20
  317.4 0.0 all-reduce.2.cloned.1.call-done
  317.5 3.0 convert_add_fusion
  320.5 0.5 multiply_convert_fusion.4
  321.0 1.3 broadcast_in_dim.44
  322.3 2.2 reshape.148
  324.5 6.3 scatter_custom_fusion
  330.8 3.6 all-to-all-start
  334.5 0.3 reduce-scatter.2.cloned.1.call-start
  334.7 3.6 bitcast_dynamic-update-slice_fusion.2
  338.4 13.7 %collective-permute-done.1 = bf16[1,512,2752]{1,2,0:T(8,128)(2,1)} collective-permute-done((bf16[1,512,2752]{1,2,0:T(8,128)(2,1)}, bf16[1,512,2752]{1,2,0:T(8,128)(2,1)}, u32[]{:S(2)}, u32[]{:S(2)}) %collective-permute-start.1) | collective-permute-done | bytes 2818080 | tf_op jit(solution)/shard_map/ppermute | solution.py:25
  352.1 3.6 bitcast_dynamic-update-slice_fusion.1
  355.7 98.5 %collective-permute-done.2 = bf16[1,512,2752]{1,2,0:T(8,128)(2,1)} collective-permute-done((bf16[1,512,2752]{1,2,0:T(8,128)(2,1)}, bf16[1,512,2752]{1,2,0:T(8,128)(2,1)}, u32[]{:S(2)}, u32[]{:S(2)}) %collective-permute-start.2) | collective-permute-done | bytes 2818080 | tf_op jit(solution)/shard_map/ppermute | solution.py:20
  454.2 3.6 bitcast_dynamic-update-slice_fusion
  457.8 0.0 all-to-all-done
  457.8 12.2 %fusion.33 = f32[576,2752]{1,0:T(8,128)} fusion(bf16[576,2048]{1,0:T(8,128)(2,1)S(1)} %bitcast.67, bf16[2048,2752]{0,1:T(8,128)(2,1)} %bitcast_dynamic-update-slice_fusion), kind=kOutput, calls=%fused_computation.56 | convolution fusion | flops 6492782592 | bytes 19972096 | tf_op jit(solution)/shard_map/dot_general | solution.py:95
  470.0 190.0 %all-gather.9.cloned.1.call-done = bf16[1,2048,2752]{1,2,0:T(8,128)(2,1)} async-done(((bf16[1,512,2752]{1,2,0:T(8,128)(2,1)}), bf16[1,2048,2752]{1,2,0:T(8,128)(2,1)}) %all-gather.9.cloned.1.call-update) | async-done | bytes 11272208 | tf_op jit(solution)/shard_map/all_gather | solution.py:92
  659.9 27.1 %fusion.13 = bf16[576,2048]{1,0:T(8,128)(2,1)} fusion(bf16[1,2048,2752]{1,2,0:T(8,128)(2,1)} %all-gather.11.cloned.1.call-done, f32[576,2752]{1,0:T(8,128)} %fusion.33, bf16[576,2048]{1,0:T(8,128)(2,1)S(1)} %bitcast.68, bf16[1,2048,2752]{1,2,0:T(8,128)(2,1)} %all-gather.9.cloned.1.call-done), kind=kOutput, calls=%fused_computation.18 | convolution fusion | flops 12996255744 | bytes 33603584 | tf_op jit(solution)/shard_map/dot_general | solution.py:98
  687.0 0.0 reduce-scatter.2.cloned.1.call-update
  687.0 8.2 %reduce-scatter.2.cloned.1.call-done = bf16[576,1024]{1,0:T(8,128)(2,1)} async-done(((bf16[576,2048]{1,0:T(8,128)(2,1)}), bf16[576,1024]{1,0:T(8,128)(2,1)}) %reduce-scatter.2.cloned.1.call-update) | async-done | bytes 1179664 | tf_op jit(solution)/shard_map/reduce_scatter | solution.py:103
  695.2 4.5 all-to-all-start.1
  699.8 0.1 copy.19
  700.0 15.7 %all-to-all-done.1 = bf16[4,144,1024]{2,1,0:T(8,128)(2,1)} async-done(((bf16[4,144,1024]{2,1,0:T(8,128)(2,1)}), bf16[4,144,1024]{2,1,0:T(8,128)(2,1)}, u32[]{:S(2)}, u32[]{:S(2)}) %all-to-all-start.1) | async-done | bytes 1179680 | tf_op jit(solution)/shard_map/all_to_all | solution.py:109
  715.6 1.5 bitcast_convert_fusion
  717.2 2.7 gather_fusion
  719.9 2.5 reshape.133
  722.5 2.6 multiply_reduce_fusion
  725.1 0.9 add_convert_fusion
  (27 shorter events, 0.1 us)
Async XLA Ops:
  7.4 40.6 %copy-start = (bf16[256,1024]{1,0:T(8,128)(2,1)S(1)}, bf16[256,1024]{1,0:T(8,128)(2,1)}, u32[]{:S(2)}) copy-start(bf16[256,1024]{1,0:T(8,128)(2,1)} %param.12) | copy-start | bytes 1572868
  7.4 40.5 %all-gather.5.cloned.1.call-start = ((), (), s32[]{:S(2)}) async-start(), calls=%async_computation.3 | async-start | bytes 2621440 | tf_op jit(solution)/shard_map/all_gather | solution.py:57
  9.5 75.6 %all-gather.7.cloned.1.call-start = ((), (), s32[]{:S(2)}) async-start(), calls=%async_computation.4 | async-start | bytes 2621440 | tf_op jit(solution)/shard_map/all_gather | solution.py:58
  10.2 307.2 %all-reduce.2.cloned.1.call-start = ((), (), s32[]{:S(2)}) async-start(), calls=%async_computation.5 | async-start | bytes 2097152 | tf_op jit(solution)/shard_map/psum | solution.py:73
  51.3 3.2 copy-start.2
  88.0 5.9 copy-start.9
  96.1 5.1 copy-start.6
  96.2 373.8 %all-gather.11.cloned.1.call-start = ((), (), s32[]{:S(2)}) async-start(), calls=%async_computation.7 | async-start | bytes 14090240 | tf_op jit(solution)/shard_map/all_gather | solution.py:93
  96.8 563.2 %all-gather.9.cloned.1.call-start = ((), (), s32[]{:S(2)}) async-start(), calls=%async_computation.6 | async-start | bytes 14090240 | tf_op jit(solution)/shard_map/all_gather | solution.py:92
  97.3 116.4 %collective-permute-start = (bf16[1,512,2752]{1,2,0:T(8,128)(2,1)}, bf16[1,512,2752]{1,2,0:T(8,128)(2,1)}, u32[]{:S(2)}, u32[]{:S(2)}) collective-permute-start(bf16[1,512,2752]{1,2,0:T(8,128)(2,1)} %param.19), channel_id=1, source_target_pairs={{0,8},{8,16},{16,24},{24,0},{1,9},{9,17},{17,25},{25,1},{2,10},{10... | collective-permute-start | bytes 8454152 | tf_op jit(solution)/shard_map/ppermute | solution.py:20
  98.9 253.2 %collective-permute-start.1 = (bf16[1,512,2752]{1,2,0:T(8,128)(2,1)}, bf16[1,512,2752]{1,2,0:T(8,128)(2,1)}, u32[]{:S(2)}, u32[]{:S(2)}) collective-permute-start(bf16[1,512,2752]{1,2,0:T(8,128)(2,1)} %param.19), channel_id=1, source_target_pairs={{0,24},{8,0},{16,8},{24,16},{1,25},{9,1},{17,9},{25,17},{2,26},{10... | collective-permute-start | bytes 8454152 | tf_op jit(solution)/shard_map/ppermute | solution.py:25
  110.5 206.9 %copy-start.7 = (bf16[2048]{0:T(1024)(128)(2,1)S(1)}, bf16[2048]{0:T(1024)(128)(2,1)}, u32[]{:S(2)}) copy-start(bf16[2048]{0:T(1024)(128)(2,1)} %param.16) | copy-start | bytes 12292
  110.5 207.0 %copy-start.4 = (bf16[256,2048]{1,0:T(8,128)(2,1)S(1)}, bf16[256,2048]{1,0:T(8,128)(2,1)}, u32[]{:S(2)}) copy-start(bf16[256,2048]{1,0:T(8,128)(2,1)} %param.11) | copy-start | bytes 3145732
  213.8 240.4 %collective-permute-start.2 = (bf16[1,512,2752]{1,2,0:T(8,128)(2,1)}, bf16[1,512,2752]{1,2,0:T(8,128)(2,1)}, u32[]{:S(2)}, u32[]{:S(2)}) collective-permute-start(bf16[1,512,2752]{1,2,0:T(8,128)(2,1)} %collective-permute-done), channel_id=1, source_target_pairs={{0,8},{8,16},{16,24},{24,0},{1,9},{9,17},{17,25},{25,1},{2,10},{10... | collective-permute-start | bytes 8454152 | tf_op jit(solution)/shard_map/ppermute | solution.py:20
  317.5 3.0 copy-start.5
  330.8 127.0 %all-to-all-start = ((bf16[4,144,2048]{2,1,0:T(8,128)(2,1)}), bf16[4,144,2048]{2,1,0:T(8,128)(2,1)S(1)}, u32[]{:S(2)}, u32[]{:S(2)}) async-start(bf16[4,144,2048]{2,1,0:T(8,128)(2,1)} %bitcast.8), calls=%async_computation | async-start | bytes 4718592 | tf_op jit(solution)/shard_map/all_to_all | solution.py:88
  334.5 360.8 %reduce-scatter.2.cloned.1.call-start = ((), (), s32[]{:S(2)}) async-start(), calls=%async_computation.8 | async-start | bytes 3538944 | tf_op jit(solution)/shard_map/reduce_scatter | solution.py:103
  687.0 12.8 %copy-start.8 = (f32[256,2]{0,1:T(2,128)S(1)}, f32[256,2]{0,1:T(2,128)}, u32[]{:S(2)}) copy-start(f32[256,2]{0,1:T(2,128)} %param.18) | copy-start | bytes 6148
  695.2 20.4 %all-to-all-start.1 = ((bf16[4,144,1024]{2,1,0:T(8,128)(2,1)}), bf16[4,144,1024]{2,1,0:T(8,128)(2,1)}, u32[]{:S(2)}, u32[]{:S(2)}) async-start(bf16[4,144,1024]{2,1,0:T(8,128)(2,1)} %bitcast.71), calls=%async_computation.2 | async-start | bytes 2359296 | tf_op jit(solution)/shard_map/all_to_all | solution.py:109
  719.9 6.2 copy-start.1
  722.4 2.7 copy-start.3
Sparse Core Ops, SparseCore 0:
  10.0 37.8 all-gather.4
  49.8 35.3 all-gather.6
  96.3 19.5 all-reduce.1
  687.1 8.0 reduce-scatter.1
Sparse Core Ops, SparseCore 1:
  98.3 366.1 all-gather.10
  466.0 193.9 all-gather.8
